TPU v7x, 32 devices: a whole 2x2x4 slice. The times are simulated.
32 devices in a mesh: row: 4 (over x, core), col: 8 (over z, y).
Axes of the slice: x: 2, y: 2, z: 4, core: 2. Of those that a mesh axis runs over, the one named last changes fastest.
Arguments:
- series: bfloat16 [512, 8192], P(None, ('row', 'col')), may hold values from -6 to 6
- lag_weight: float32 [4], replicated, may hold values from 0.25 to 1
- start_basis: bfloat16 [64, 8192], P(None, ('row', 'col')), may hold values from -5.25 to 5.25
- block_pairs: int32 [4, 8, 32, 2], P('row', 'col'), may hold values from 0 to 31, as said below
- pair_count: int32 [4, 8], P('row', 'col'), may hold values from 1 to 32, as said below
Outputs:
- basis: float32 [64, 8192], P(None, ('row', 'col'))
- rayleigh: float32 [64, 64], replicated
Inputs may be any that keep to these rules, and one draw needn't show every extreme that they name: For every slot s of device (r, c), block_pairs[r, c, s, 0] is a block of row group r, from r * 8 to (r + 1) * 8 - 1, and block_pairs[r, c, s, 1] is a block held by a device of mesh column c: (block_pairs[r, c, s, 1]) mod (8) equals c. Slots that are not live hold blocks of the same ranges and are no part of the network. `pair_count`: the number of live slots of device (r, c); some device has exactly 32.
All inputs are finite; a program needn't handle non-finite values.
Results may differ from a plain program's by a relative error of at most 0.0045.
Values may be sent and summed in bfloat16 or wider, within the bound.
A program may use at most 64 MiB of HBM per device.

v0:
```python
import math

import jax
import jax.numpy as jnp
from jax import lax
from jax.sharding import PartitionSpec as P

BLOCK = 256
ITERS = 2


BETA_CORR = 8.0
GRAM_EPS = 1e-05
HIGHEST = lax.Precision.HIGHEST


def lagged_tile(lead_block, trail_block, lag_weight, tile_scale):
    day_count = lead_block.shape[0]
    block_width = lead_block.shape[1]
    lag_count = lag_weight.shape[0]
    zero_rows = jnp.zeros((lag_count, block_width), lead_block.dtype)
    lead_padded = jnp.concatenate([lead_block, zero_rows], axis=0)
    trail_padded = jnp.concatenate([trail_block, zero_rows], axis=0)
    lead_shifted = jnp.concatenate(
        [lead_padded[offset : offset + day_count] for offset in range(lag_count)], axis=1
    )
    trail_shifted = jnp.concatenate(
        [trail_padded[offset : offset + day_count] for offset in range(lag_count)], axis=1
    )
    contract = (((0,), (0,)), ((), ()))
    forward = lax.dot_general(
        lead_shifted, trail_block, contract, preferred_element_type=jnp.float32
    )
    backward = lax.dot_general(
        lead_block, trail_shifted, contract, preferred_element_type=jnp.float32
    )
    forward = forward.reshape(lag_count, block_width, block_width)
    backward = jnp.transpose(backward.reshape(block_width, lag_count, block_width), (1, 0, 2))
    soft_corr = jnp.tanh(BETA_CORR / day_count * (forward + backward))
    weighted = jnp.sum(lag_weight[:, None, None] * soft_corr, axis=0)
    return (tile_scale * weighted).astype(jnp.bfloat16)


def local(series, lag_weight, start_basis, block_pairs, pair_count):
    n_rows = lax.axis_size("row")
    n_cols = lax.axis_size("col")
    row_index = lax.axis_index("row")
    local_cells = series.shape[1]
    local_blocks = local_cells // BLOCK
    row_blocks = local_blocks * n_cols
    col_blocks = local_blocks * n_rows
    slot_total = block_pairs.shape[2]
    cell_total = local_cells * n_rows * n_cols
    rank_size = start_basis.shape[0]
    tile_scale = 0.25 / math.sqrt(BLOCK)
    row_series = lax.all_gather(series, "col", axis=1, tiled=True)
    col_series = lax.all_gather(series, "row", axis=1, tiled=True)
    slot_pairs = block_pairs.reshape(slot_total, 2)
    slot_count = pair_count.reshape(1)
    row_first = row_index * row_blocks
    slot_ids = jnp.arange(slot_total, dtype=jnp.int32)
    own_rows = slot_pairs[:, 0] - row_first
    global_block = slot_pairs[:, 1]
    own_cols = global_block // local_blocks // n_cols * local_blocks + global_block % local_blocks
    built_count = slot_count[0]
    tile_rows = own_rows
    tile_cols = own_cols
    tile_rows = jnp.clip(tile_rows, 0, row_blocks - 1)
    tile_cols = jnp.clip(tile_cols, 0, col_blocks - 1)
    live_slots = slot_ids < built_count

    def build_one(slot, tiles):
        lead_block = lax.dynamic_slice_in_dim(row_series, tile_rows[slot] * BLOCK, BLOCK, 1)
        trail_block = lax.dynamic_slice_in_dim(col_series, tile_cols[slot] * BLOCK, BLOCK, 1)
        tile = lagged_tile(lead_block, trail_block, lag_weight, tile_scale)
        return lax.dynamic_update_index_in_dim(tiles, tile, slot, 0)

    tiles = lax.fori_loop(
        0, built_count, build_one, jnp.zeros((slot_total, BLOCK, BLOCK), jnp.bfloat16)
    )
    live_float = live_slots.astype(jnp.float32)[:, None]
    row_onehot = (tile_rows[:, None] == jnp.arange(row_blocks, dtype=jnp.int32)[None, :]).astype(
        jnp.float32
    ) * live_float
    col_onehot = (tile_cols[:, None] == jnp.arange(col_blocks, dtype=jnp.int32)[None, :]).astype(
        jnp.float32
    ) * live_float

    def project(basis_now):
        row_basis = lax.all_gather(basis_now, "col", axis=1, tiled=True).reshape(
            rank_size, row_blocks, BLOCK
        )
        col_basis = lax.all_gather(basis_now, "row", axis=1, tiled=True)
        col_basis = col_basis.reshape(rank_size, col_blocks, BLOCK)
        lead_basis = jnp.take(row_basis, tile_rows, axis=1)
        trail_basis = jnp.take(col_basis, tile_cols, axis=1)
        into_cols = jnp.einsum(
            "ksa,sab->ksb", lead_basis, tiles, preferred_element_type=jnp.float32
        )
        return (trail_basis, into_cols)

    current = start_basis
    basis = start_basis.astype(jnp.float32)
    for iteration in range(ITERS):
        network_trail_basis, network_into_cols = project(current)
        into_rows = jnp.einsum(
            "ksb,sab->ksa", network_trail_basis, tiles, preferred_element_type=jnp.float32
        )
        row_part = jnp.einsum("ksa,sr->kra", into_rows, row_onehot, precision=HIGHEST)
        row_part = row_part.reshape(rank_size, row_blocks * BLOCK)
        col_part = jnp.einsum("ksb,sr->krb", network_into_cols, col_onehot, precision=HIGHEST)
        col_part = col_part.reshape(rank_size, col_blocks * BLOCK)
        row_total = lax.psum_scatter(row_part, "col", scatter_dimension=1, tiled=True)
        col_total = lax.psum_scatter(col_part, "row", scatter_dimension=1, tiled=True)
        product = row_total + col_total
        local_gram = jnp.dot(product, product.T, precision=HIGHEST)
        gram = lax.psum(local_gram, ("row", "col")) / cell_total
        gram = gram + GRAM_EPS * jnp.eye(rank_size, dtype=jnp.float32)
        lower = jnp.linalg.cholesky(gram)
        basis = lax.linalg.triangular_solve(lower, product, left_side=True, lower=True)
        current = basis.astype(jnp.bfloat16)
    trail_basis, into_cols = project(current)
    masked_cols = into_cols * live_float[None, :, :]
    local_form = jnp.einsum(
        "ksb,lsb->kl", masked_cols, trail_basis.astype(jnp.float32), precision=HIGHEST
    )
    local_form = local_form + local_form.T
    rayleigh = lax.psum(local_form, ("row", "col")) / cell_total
    return (basis, rayleigh)


def solution(mesh):
    return jax.shard_map(
        local,
        mesh=mesh,
        in_specs=(
            P(None, ("row", "col")),
            P(),
            P(None, ("row", "col")),
            P("row", "col", None, None),
            P("row", "col"),
        ),
        out_specs=(P(None, ("row", "col")), P()),
        check_vma=False,
    )
```

profile of v0, /device:TPU:14, one launch (start us, length us, event | category | flops | bytes accessed | tf_op | source)
XLA Modules:
  0.0 704.8 jit_solution(5229040905246252676)
XLA Ops:
  7.2 0.7 all-gather.5.cloned.1.call-update
  7.9 0.7 all-gather.3.cloned.1.call-update
  8.7 5.6 all_gather.26
  15.0 28.6 %all_gather.27 = bf16[64,2048]{1,0:T(8,128)(2,1)S(1)} all-gather(bf16[64,256]{1,0:T(8,128)(2,1)} %param.16), channel_id=1, replica_groups=mesh['row'=4,'col'=8] {'col'}, dimensions={1}, use_global_device_ids=true | all-gather | bytes 294912 | tf_op jit(solution)/shard_map/all_gather | solution.py:90
  43.6 0.8 compare_and_fusion
  45.8 32.6 %all-gather.3.cloned.1.call-done = bf16[512,2048]{1,0:T(8,128)(2,1)} async-done(((bf16[512,256]{1,0:T(8,128)(2,1)}), bf16[512,2048]{1,0:T(8,128)(2,1)}) %all-gather.3.cloned.1.call-update) | async-done | bytes 2097168 | tf_op jit(solution)/shard_map/all_gather | solution.py:56
  78.4 2.4 broadcast_in_dim.30
  80.8 64.7 %while.10 = (s32[]{:T(128)}, bf16[32,256,256]{2,1,0:T(8,128)(2,1)}, s32[]{:T(128)}, f32[4]{0:T(128)S(1)}, s32[32]{0:T(128)S(1)}, /*index=5*/bf16[512,2048]{1,0:T...) while((s32[]{:T(128)}, bf16[32,256,256]{2,1,0:T(8,128)(2,1)}, ...), condition=%wide.region_2.3_spmd, body=%wide.region_0.2_spmd.sunk | while | flops 546373632 | bytes 10617143 | solution.py:78
  83.9 1.1 constant_dynamic-slice_fusion.3
  86.5 0.7 fusion.134
  90.3 1.1 constant_dynamic-slice_fusion.3
  92.9 0.7 fusion.134
  96.7 1.1 constant_dynamic-slice_fusion.3
  99.3 0.7 fusion.134
  103.1 1.1 constant_dynamic-slice_fusion.3
  105.7 0.7 fusion.134
  109.6 1.1 constant_dynamic-slice_fusion.3
  112.1 0.7 fusion.134
  116.0 1.1 constant_dynamic-slice_fusion.3
  118.5 0.7 fusion.134
  122.4 1.1 constant_dynamic-slice_fusion.3
  124.9 0.7 fusion.134
  128.8 1.1 constant_dynamic-slice_fusion.3
  131.3 0.7 fusion.134
  135.2 1.1 constant_dynamic-slice_fusion.3
  137.8 0.7 fusion.134
  141.6 1.1 constant_dynamic-slice_fusion.3
  144.2 0.7 fusion.134
  145.5 3.1 convolution_bitcast_fusion.1
  148.6 2.2 fusion.31
  150.8 0.8 copy.52
  151.6 3.6 convolution_bitcast_fusion.3
  155.2 2.2 fusion.33
  157.5 1.0 copy.51
  158.5 153.2 %reduce-scatter.7.cloned.1.call-done = f32[64,256]{1,0:T(8,128)} async-done(((f32[64,1024]{1,0:T(8,128)}), f32[64,256]{1,0:T(8,128)}) %reduce-scatter.7.cloned.1.call-update) | async-done | bytes 65552 | tf_op jit(solution)/shard_map/reduce_scatter | solution.py:114
  311.6 66.8 %reduce-scatter.5.cloned.1.call-done = f32[64,256]{1,0:T(8,128)} async-done(((f32[64,2048]{1,0:T(8,128)}), f32[64,256]{1,0:T(8,128)}) %reduce-scatter.5.cloned.1.call-update) | async-done | bytes 65552 | tf_op jit(solution)/shard_map/reduce_scatter | solution.py:113
  378.4 0.9 add.82
  379.5 39.6 %psum.21 = f32[64,64]{0,1:T(8,128)S(1)} all-reduce(f32[64,64]{0,1:T(8,128)S(1)} %fusion.104), channel_id=1, replica_groups=mesh['row'=4,'col'=8] {'row','col'}, use_global_device_ids=true, to_apply=%region_5.8 | all-reduce | flops 4096 | bytes 32768 | tf_op jit(solution)/shard_map/psum | solution.py:117
  419.2 5.8 cholesky.44
  425.1 0.6 compare_reduce_fusion.1
  425.7 0.7 fusion.62
  426.4 4.9 custom-call.6
  431.5 27.1 %all_gather.29 = bf16[64,2048]{1,0:T(8,128)(2,1)S(1)} all-gather(bf16[64,256]{1,0:T(8,128)(2,1)S(1)} %convolution_convert_fusion), channel_id=1, replica_groups=mesh['row'=4,'col'=8] {'col'}, dimensions={1}, use_global_device_ids=true | all-gather | bytes 294912 | tf_op jit(solution)/shard_map/all_gather | solution.py:90
  458.7 5.4 all_gather.28
  464.7 3.1 convolution_bitcast_fusion
  467.8 2.2 fusion.27
  470.0 0.8 copy.54
  471.5 3.6 convolution_bitcast_fusion.2
  475.1 2.2 fusion.29
  477.3 1.0 copy.53
  478.3 15.6 %reduce-scatter.11.cloned.1.call-done = f32[64,256]{1,0:T(8,128)} async-done(((f32[64,1024]{1,0:T(8,128)}), f32[64,256]{1,0:T(8,128)}) %reduce-scatter.11.cloned.1.call-update) | async-done | bytes 65552 | tf_op jit(solution)/shard_map/reduce_scatter | solution.py:114
  493.9 66.7 %reduce-scatter.9.cloned.1.call-done = f32[64,256]{1,0:T(8,128)} async-done(((f32[64,2048]{1,0:T(8,128)}), f32[64,256]{1,0:T(8,128)}) %reduce-scatter.9.cloned.1.call-update) | async-done | bytes 65552 | tf_op jit(solution)/shard_map/reduce_scatter | solution.py:113
  560.6 0.9 add.84
  561.7 39.6 %psum.22 = f32[64,64]{0,1:T(8,128)S(1)} all-reduce(f32[64,64]{0,1:T(8,128)S(1)} %fusion.105), channel_id=1, replica_groups=mesh['row'=4,'col'=8] {'row','col'}, use_global_device_ids=true, to_apply=%region_10.15 | all-reduce | flops 4096 | bytes 32768 | tf_op jit(solution)/shard_map/psum | solution.py:117
  601.4 5.8 cholesky.55
  607.9 0.7 fusion.63
  608.6 4.9 custom-call.7
  613.5 0.9 fusion.103
  614.4 27.2 %all_gather.30 = bf16[64,2048]{1,0:T(8,128)(2,1)S(1)} all-gather(bf16[64,256]{1,0:T(8,128)(2,1)S(1)} %get-tuple-element.86), channel_id=1, replica_groups=mesh['row'=4,'col'=8] {'col'}, dimensions={1}, use_global_device_ids=true | all-gather | bytes 294912 | tf_op jit(solution)/shard_map/all_gather | solution.py:90
  641.6 5.4 all_gather.31
  647.6 3.1 fusion.37
  651.3 1.3 fusion.25
  652.7 44.5 %psum.23 = f32[64,64]{0,1:T(8,128)S(1)} all-reduce(f32[64,64]{0,1:T(8,128)S(1)} %bitcast_add_fusion), channel_id=1, replica_groups=mesh['row'=4,'col'=8] {'row','col'}, use_global_device_ids=true, to_apply=%region_11.16 | all-reduce | flops 4096 | bytes 32768 | tf_op jit(solution)/shard_map/psum | solution.py:128
  697.2 0.7 copy.41
  (118 shorter events, 32.3 us)
Async XLA Ops:
  7.2 38.6 %all-gather.5.cloned.1.call-start = ((), (), s32[]{:S(2)}) async-start(), calls=%async_computation.5 | async-start | bytes 1310720 | tf_op jit(solution)/shard_map/all_gather | solution.py:57
  7.9 70.5 %all-gather.3.cloned.1.call-start = ((), (), s32[]{:S(2)}) async-start(), calls=%async_computation.4 | async-start | bytes 2359296 | tf_op jit(solution)/shard_map/all_gather | solution.py:56
  8.6 303.0 %reduce-scatter.7.cloned.1.call-start = ((), (), s32[]{:S(2)}) async-start(), calls=%async_computation.7 | async-start | bytes 327680 | tf_op jit(solution)/shard_map/reduce_scatter | solution.py:114
  44.4 1.3 copy-start.1
  78.4 2.4 copy-start
  151.6 226.8 %reduce-scatter.5.cloned.1.call-start = ((), (), s32[]{:S(2)}) async-start(), calls=%async_computation.6 | async-start | bytes 589824 | tf_op jit(solution)/shard_map/reduce_scatter | solution.py:113
  158.4 335.4 %reduce-scatter.11.cloned.1.call-start = ((), (), s32[]{:S(2)}) async-start(), calls=%async_computation.9 | async-start | bytes 327680 | tf_op jit(solution)/shard_map/reduce_scatter | solution.py:114
  470.8 89.8 %reduce-scatter.9.cloned.1.call-start = ((), (), s32[]{:S(2)}) async-start(), calls=%async_computation.8 | async-start | bytes 589824 | tf_op jit(solution)/shard_map/reduce_scatter | solution.py:113
Sparse Core Ops, SparseCore 0:
  9.5 17.0 all-gather.4
  28.6 49.6 all-gather.2
  151.7 159.8 reduce-scatter.6
  315.2 63.1 reduce-scatter.4
  470.9 22.9 reduce-scatter.10
  497.4 63.1 reduce-scatter.8
where the time goes:
time: 706 us; the launch traced here: 705 us
  waiting for transfers between devices  336 us (48%)
  blocking collectives  223 us (32%)
  matrix products  37.4 us (5%)
  local copies, waits for them, and re-layouts  36.2 us (5%)
  other arithmetic  35.8 us (5%)
  loops' own time  20.8 us (3%)
  between operations  15.1 us (2%)
    reduce_scatter x2, waiting for transfers between devices, local(): lax.psum_scatter(col_part, 'row', scatter_dimension=1, tiled=True)  169 us
    reduce_scatter x2, waiting for transfers between devices, local(): lax.psum_scatter(row_part, 'col', scatter_dimension=1, tiled=True)  133 us
    all_gather x3, blocking collectives, project(): lax.all_gather(basis_now, 'col', axis=1, tiled=True)  82.9 us
    psum x2, blocking collectives, local(): gram = lax.psum(local_gram, ('row', 'col')) / cell_total  79.1 us
    psum x1, blocking collectives, local(): rayleigh = lax.psum(local_form, ('row', 'col')) / cell_total  44.5 us
    all_gather x1, waiting for transfers between devices, local(): row_series = lax.all_gather(series, 'col', axis=1, tiled=True)  32.6 us
    another operation x1, loops' own time, local(): lax.fori_loop(0, built_count, build_one, jnp.zeros((slot_total, BLOCK, BL...  20.8 us
    all_gather x3, blocking collectives, project(): col_basis = lax.all_gather(basis_now, 'row', axis=1, tiled=True)  16.5 us
  transfers between devices with their start and end apart: 6, of which 5 were waited for; matrix products, arithmetic and copies ran while one was open for 2% of the time, Pallas kernels for 0%

commit v1 on v0

--- a/solution.py
+++ b/solution.py
@@ -3,6 +3,8 @@
 import jax
 import jax.numpy as jnp
 from jax import lax
+from jax.experimental import pallas as pl
+from jax.experimental.pallas import tpu as pltpu
 from jax.sharding import PartitionSpec as P
 
 BLOCK = 256
@@ -129,9 +131,345 @@
     return (basis, rayleigh)
 
 
+VMEM_BYTES = 48 * 2**20
+MESH = pl.DeviceIdType.MESH
+NT = (((1,), (1,)), ((), ()))
+
+
+def pack(square):
+    quarter = square.shape[0] // 4
+    return jnp.concatenate([square[i * quarter : (i + 1) * quarter] for i in range(4)], axis=1)
+
+
+def unpack(packed):
+    width = packed.shape[1] // 4
+    return jnp.concatenate([packed[:, i * width : (i + 1) * width] for i in range(4)], axis=0)
+
+
+def inverse_factor(gram):
+    size = gram.shape[0]
+    rows = lax.broadcasted_iota(jnp.int32, (size, size), 0)
+    lanes = lax.broadcasted_iota(jnp.int32, (size, size), 1)
+    both = jnp.concatenate([gram, (rows == lanes).astype(jnp.float32)], axis=1)
+    groups = [both[i : i + 8] for i in range(0, size, 8)]
+    row_ids = lax.broadcasted_iota(jnp.int32, (8, 1), 0)
+    for k in range(size):
+        home = k // 8
+        pivot_row = groups[home][k % 8 : k % 8 + 1]
+        scaled_row = pivot_row * (1.0 / pivot_row[:, k : k + 1])
+        for g in range(home, len(groups)):
+            column = groups[g][:, k : k + 1]
+            if g == home:
+                column = jnp.where(row_ids > k % 8, column, 0.0)
+            groups[g] = groups[g] - column * scaled_row
+    both = jnp.concatenate(groups, axis=0)
+    pivots = jnp.sum(jnp.where(rows == lanes, both[:, :size], 0.0), axis=1, keepdims=True)
+    return both[:, size:] / jnp.sqrt(pivots)
+
+
+def kernel(
+    n_rows, n_cols, days, rank, lags,
+    own_ref, weight_ref, basis_ref, rayleigh_ref,
+    held, tiles, stack, dots, parts, forms, counts, send_sem, recv_sem,
+):
+    n_blocks = n_rows * n_cols
+    depth = n_cols // 2
+    half = n_blocks // 2
+    width = own_ref.shape[1]
+    chunk = width // 2
+    cells = n_blocks * width
+    tile_scale = 0.25 / math.sqrt(width)
+    row, col = lax.axis_index("row"), lax.axis_index("col")
+    x, core = row // 2, lax.rem(row, 2)
+    z, y = col // 2, lax.rem(col, 2)
+    me = row * n_cols + col
+
+    def place(flip_a, flip_b, other, far):
+        side = lax.rem(core + other, 2)
+        flip_x = flip_a * (1 - side) + flip_b * side
+        flip_y = flip_b * (1 - side) + flip_a * side
+        at_x, at_y = lax.rem(x + flip_x, 2), lax.rem(y + flip_y, 2)
+        at_z = lax.rem(z + far, depth)
+        return at_x * 2 + side, at_z * 2 + at_y
+
+    def block_of(s):
+        at_row, at_col = place(
+            lax.rem(s // depth, 2), lax.rem(s // (2 * depth), 2), s // half, lax.rem(s, depth)
+        )
+        return at_row * n_cols + at_col
+
+    peer_a = (lax.rem(x + 1 - core, 2) * 2 + core, z * 2 + lax.rem(y + core, 2))
+    peer_b = (lax.rem(x + core, 2) * 2 + core, z * 2 + lax.rem(y + 1 - core, 2))
+    sibling = (x * 2 + 1 - core, col)
+    line = [(row, lax.rem(z + far, depth) * 2 + y) for far in range(1, depth)]
+
+    barrier = pltpu.get_barrier_semaphore()
+    for peer in line + [peer_a, peer_b, sibling]:
+        pl.semaphore_signal(barrier, inc=1, device_id=peer, device_id_type=MESH)
+    own = own_ref[...]
+    held[me] = own
+    pl.semaphore_wait(barrier, len(line) + 3)
+
+    first_a, first_b, first_s = depth - 1, 2 * depth - 1, 4 * depth - 1
+
+    def copy(step, buffer, block, send, recv, peer):
+        return pltpu.make_async_remote_copy(
+            src_ref=buffer.at[block],
+            dst_ref=buffer.at[block],
+            send_sem=send_sem.at[step, send],
+            recv_sem=recv_sem.at[step, recv],
+            device_id=peer,
+            device_id_type=MESH,
+        )
+
+    def forward(step, buffer, k):
+        block = block_of(k)
+
+        @pl.when(k < depth)
+        def _():
+            copy(step, buffer, block, first_a + k, depth + k, peer_a).start()
+
+        @pl.when(k < 2 * depth)
+        def _():
+            copy(step, buffer, block, first_b + k, 2 * depth + k, peer_b).start()
+
+        copy(step, buffer, block, first_s + k, half + k, sibling).start()
+
+    def begin(step, buffer):
+        for far in range(1, depth):
+            copy(step, buffer, me, far - 1, depth - far, line[far - 1]).start()
+        forward(step, buffer, 0)
+
+    def arrive(step, buffer, s):
+        copy(step, buffer, block_of(s), 0, s, sibling).wait_recv()
+
+    def gather(step, buffer, use, carry):
+        carry = use(me, carry)
+        arrive(step, buffer, half)
+        carry = use(block_of(half), carry)
+
+        def body(k, carry):
+            arrive(step, buffer, k)
+            forward(step, buffer, k)
+            carry = use(block_of(k), carry)
+            arrive(step, buffer, half + k)
+            return use(block_of(half + k), carry)
+
+        return lax.fori_loop(1, half, body, carry)
+
+    begin(0, held)
+    lanes = lax.broadcasted_iota(jnp.int32, (width, days), 1)
+    turned = own[:days].astype(jnp.float32).T
+    shifted = [turned]
+    for lag in range(1, lags):
+        shifted.append(jnp.where(lanes < days - lag, pltpu.roll(turned, days - lag, 1), 0.0))
+        shifted.append(jnp.where(lanes >= lag, pltpu.roll(turned, lag, 1), 0.0))
+    shifts = len(shifted)
+    for i, part in enumerate(shifted):
+        for q in range(2):
+            stack[q, i * chunk : (i + 1) * chunk, :] = part[q * chunk : (q + 1) * chunk].astype(
+                jnp.bfloat16
+            )
+    weights = [weight_ref[lag] for lag in range(lags)]
+
+    def build(block, carry):
+        series = held[block, 0:days, :]
+        for q in range(2):
+            sums = jnp.dot(stack[q], series, preferred_element_type=jnp.float32)
+            rows = [sums[i * chunk : (i + 1) * chunk] for i in range(shifts)]
+            total = weights[0] * jnp.tanh(2 * BETA_CORR / days * rows[0])
+            for lag in range(1, lags):
+                total += weights[lag] * jnp.tanh(
+                    BETA_CORR / days * (rows[2 * lag - 1] + rows[2 * lag])
+                )
+            tiles[block, q * chunk : (q + 1) * chunk, :] = (tile_scale * total).astype(
+                jnp.bfloat16
+            )
+        dots[block] = lax.dot_general(
+            held[block, days : days + rank, :], tiles[block], NT, preferred_element_type=jnp.float32
+        )
+        return carry
+
+    gather(0, held, build, jnp.int32(0))
+
+    count_rows = counts.shape[0]
+
+    def add_counts(block, total):
+        return total + held[block, days + rank : days + rank + count_rows, :].astype(jnp.float32)
+
+    zero_counts = jnp.zeros((count_rows, width), jnp.float32)
+    total = lax.fori_loop(0, n_blocks, add_counts, zero_counts)
+    count_lanes = lax.broadcasted_iota(jnp.int32, (count_rows, width), 1)
+    mine = jnp.sum(jnp.where(count_lanes == me, total, 0.0), axis=1, keepdims=True)
+    counts[...] = jnp.broadcast_to(mine, (count_rows, width))
+
+    zero = jnp.zeros((rank, width), jnp.float32)
+    product = lax.fori_loop(
+        0, n_blocks, lambda b, acc: acc + counts[pl.ds(b, 1), :] * dots[b], zero
+    )
+
+    inverse = None
+    for step in range(ITERS):
+        buffer = parts.at[step]
+        buffer[me, 0:rank, :] = product
+        local_gram = lax.dot_general(
+            product, product, NT, precision=HIGHEST, preferred_element_type=jnp.float32
+        )
+        buffer[me, rank : rank + rank // 4, :] = pack(local_gram)
+        begin(step + 1, buffer)
+
+        def multiply(block, acc):
+            part = buffer[block, 0:rank, :]
+            high = part.astype(jnp.bfloat16)
+            rest = part - high.astype(jnp.float32)
+            middle = rest.astype(jnp.bfloat16)
+            low = (rest - middle.astype(jnp.float32)).astype(jnp.bfloat16)
+            split = jnp.concatenate([high, middle, low], axis=0)
+            out = lax.dot_general(split, tiles[block], NT, preferred_element_type=jnp.float32)
+            out = out[:rank] + (out[rank : 2 * rank] + out[2 * rank :])
+            return acc + counts[pl.ds(block, 1), :] * out
+
+        onward = gather(step + 1, buffer, multiply, zero)
+
+        if step == ITERS - 1:
+            local_form = lax.dot_general(
+                onward, product, NT, precision=HIGHEST, preferred_element_type=jnp.float32
+            )
+            forms[me] = pack(local_form)
+            begin(ITERS + 1, forms)
+
+        zero_packed = jnp.zeros((rank // 4, width), jnp.float32)
+        packed = lax.fori_loop(
+            0,
+            n_blocks,
+            lambda b, acc: acc + buffer[b, rank : rank + rank // 4, :],
+            zero_packed,
+        )
+        eye_rows = lax.broadcasted_iota(jnp.int32, (rank, rank), 0)
+        eye_lanes = lax.broadcasted_iota(jnp.int32, (rank, rank), 1)
+        eye = (eye_rows == eye_lanes).astype(jnp.float32)
+        inverse = inverse_factor(unpack(packed) / cells + GRAM_EPS * eye)
+        if step == ITERS - 1:
+            basis_ref[...] = jnp.dot(
+                inverse, product, precision=HIGHEST, preferred_element_type=jnp.float32
+            )
+        else:
+            product = jnp.dot(
+                inverse, onward, precision=HIGHEST, preferred_element_type=jnp.float32
+            )
+
+    gather(ITERS + 1, forms, lambda block, carry: carry, jnp.int32(0))
+    packed = lax.fori_loop(0, n_blocks, lambda b, acc: acc + forms[b], zero_packed)
+    left = jnp.dot(
+        inverse, unpack(packed), precision=HIGHEST, preferred_element_type=jnp.float32
+    )
+    rayleigh_ref[...] = (
+        lax.dot_general(left, inverse, NT, precision=HIGHEST, preferred_element_type=jnp.float32)
+        / cells
+    )
+
+    for step in range(ITERS + 2):
+        buffer = held if step == 0 else forms if step == ITERS + 1 else parts.at[step - 1]
+
+        def drain(i, carry):
+            copy(step, buffer, me, i, 0, sibling).wait_send()
+            return carry
+
+        lax.fori_loop(0, n_blocks - 1, drain, jnp.int32(0))
+
+
+def sizes(mesh_rows, mesh_cols, series, start_basis):
+    n_blocks = mesh_rows * mesh_cols
+    days, width = series
+    rank = start_basis[0]
+    count_rows = -(-n_blocks // 16) * 16
+    return n_blocks, days, width, rank, count_rows, days + rank + count_rows
+
+
+def scratch(mesh_rows, mesh_cols, series, start_basis, lags):
+    n_blocks, days, width, rank, count_rows, held_rows = sizes(
+        mesh_rows, mesh_cols, series, start_basis
+    )
+    return [
+        ((n_blocks, held_rows, width), jnp.bfloat16),
+        ((n_blocks, width, width), jnp.bfloat16),
+        ((2, (2 * lags - 1) * width // 2, days), jnp.bfloat16),
+        ((n_blocks, rank, width), jnp.float32),
+        ((ITERS, n_blocks, rank + rank // 4, width), jnp.float32),
+        ((n_blocks, rank // 4, width), jnp.float32),
+        ((count_rows, width), jnp.float32),
+    ]
+
+
+def fused(series, lag_weight, start_basis, block_pairs, pair_count):
+    n_rows, n_cols = lax.axis_size("row"), lax.axis_size("col")
+    n_blocks, days, width, rank, count_rows, held_rows = sizes(
+        n_rows, n_cols, series.shape, start_basis.shape
+    )
+    slot_total = block_pairs.shape[2]
+    slot_pairs = block_pairs.reshape(slot_total, 2)
+    live = (jnp.arange(slot_total, dtype=jnp.int32) < pair_count.reshape(1)[0])[:, None]
+    ids = jnp.arange(n_blocks, dtype=jnp.int32)[None, :]
+    leads = ((slot_pairs[:, :1] == ids) & live).astype(jnp.bfloat16)
+    trails = (slot_pairs[:, 1:] == ids).astype(jnp.bfloat16)
+    first = lax.dot_general(
+        jnp.concatenate([leads, trails * live.astype(jnp.bfloat16)], axis=0),
+        jnp.concatenate([trails, leads], axis=0),
+        (((0,), (0,)), ((), ())),
+        preferred_element_type=jnp.float32,
+    )
+    pair_counts = jnp.pad(
+        first.astype(jnp.bfloat16), ((0, count_rows - n_blocks), (0, width - n_blocks))
+    )
+    own = jnp.concatenate([series, start_basis, pair_counts], axis=0)
+    lags = lag_weight.shape[0]
+    shapes = scratch(n_rows, n_cols, series.shape, start_basis.shape, lags)
+
+    def body(*refs):
+        kernel(n_rows, n_cols, days, rank, lags, *refs)
+
+    return pl.pallas_call(
+        body,
+        out_shape=(
+            jax.ShapeDtypeStruct((rank, width), jnp.float32),
+            jax.ShapeDtypeStruct((rank, rank), jnp.float32),
+        ),
+        in_specs=[
+            pl.BlockSpec(memory_space=pltpu.VMEM),
+            pl.BlockSpec(memory_space=pltpu.SMEM),
+        ],
+        out_specs=(
+            pl.BlockSpec(memory_space=pltpu.VMEM),
+            pl.BlockSpec(memory_space=pltpu.VMEM),
+        ),
+        scratch_shapes=[pltpu.VMEM(shape, kind) for shape, kind in shapes]
+        + [
+            pltpu.SemaphoreType.DMA((ITERS + 2, n_blocks - 1)),
+            pltpu.SemaphoreType.DMA((ITERS + 2, n_blocks)),
+        ],
+        compiler_params=pltpu.CompilerParams(
+            collective_id=0, has_side_effects=True, vmem_limit_bytes=VMEM_BYTES
+        ),
+        name="subspace",
+    )(own, lag_weight)
+
+
+def either(n_rows, n_cols):
+    def run(series, lag_weight, start_basis, block_pairs, pair_count):
+        shapes = scratch(n_rows, n_cols, series.shape, start_basis.shape, lag_weight.shape[0])
+        held_bytes = sum(math.prod(s) * jnp.dtype(kind).itemsize for s, kind in shapes)
+        fits = held_bytes <= VMEM_BYTES * 3 // 4
+        one_block = series.shape[1] == BLOCK and n_rows * n_cols <= BLOCK
+        if fits and one_block and n_rows == 2 * 2 and n_cols % 2 == 0:
+            return fused(series, lag_weight, start_basis, block_pairs, pair_count)
+        return local(series, lag_weight, start_basis, block_pairs, pair_count)
+
+    return run
+
+
 def solution(mesh):
     return jax.shard_map(
-        local,
+        either(mesh.shape["row"], mesh.shape["col"]),
         mesh=mesh,
         in_specs=(
             P(None, ("row", "col")),

time: 706 us -> 161 us (0.23)
  waiting for transfers between devices: 336 us -> 0 us
  blocking collectives: 223 us -> 0 us
  Pallas kernels: 0 us -> 154 us
  matrix products: 37.4 us -> 0.17 us
  other arithmetic: 35.8 us -> 1.15 us
  local copies, waits for them, and re-layouts: 36.2 us -> 2.42 us
  loops' own time: 20.8 us -> 0 us
  between operations: 15.1 us -> 1.33 us
    reduce_scatter x4 -> x0, waiting for transfers between devices: 302 us -> none  [the longest x2 169 us: local(): lax.psum_scatter(col_part, 'row', scatter_dimension=1, tiled=True)]
    pallas_call x0 -> x1, Pallas kernels: none -> 154 us  [fused(): pl.pallas_call(body, out_shape=(jax.ShapeDtypeStruct((rank, width), jnp.f...]
    psum x3 -> x0, blocking collectives: 124 us -> none  [the longest x2 79.1 us: local(): gram = lax.psum(local_gram, ('row', 'col')) / cell_total]
    all_gather x6 -> x0, blocking collectives: 99.3 us -> none  [the longest x3 82.9 us: project(): lax.all_gather(basis_now, 'col', axis=1, tiled=True)]
    dot_general x32 -> x1, matrix products: 36.3 us -> 0.17 us  [fused(): lax.dot_general(jnp.concatenate([leads, trails * live.astype(jnp.bfloat16...]
    all_gather x2 -> x0, waiting for transfers between devices: 32.6 us -> none  [the longest x1 32.6 us: local(): row_series = lax.all_gather(series, 'col', axis=1, tiled=True)]
    another operation x10 -> x0, other arithmetic: 24.1 us -> none  [the longest x6 13 us: local(): lower = jnp.linalg.cholesky(gram)]
    dynamic_slice x30 -> x0, local copies, waits for them, and re-layouts: 22.5 us -> none  [the longest x10 10.8 us: build_one(): lax.dynamic_slice_in_dim(col_series, tile_cols[slot] * BLOCK, BLOCK, 1)]
  transfers between devices with their start and end apart: 6 -> 0, of which waited for: 5 -> 0; matrix products, arithmetic and copies ran while one was open for 2% -> 0% of each run, Pallas kernels for 0% -> 0%
where the time goes in v1:
time: 161 us; the launch traced here: 159 us
  Pallas kernels  154 us (96%)
  local copies, waits for them, and re-layouts  2.42 us (2%)
    pallas_call x1, Pallas kernels, fused(): pl.pallas_call(body, out_shape=(jax.ShapeDtypeStruct((rank, width), jnp.f...  154 us

profile of v1, /device:TPU:14, one launch (start us, length us, event | category | flops | bytes accessed | tf_op | source)
XLA Modules:
  0.0 158.7 jit_solution(12543142834659905790)
XLA Ops:
  1.3 0.0 copy-start.2
  1.3 0.7 copy-done.2
  2.0 0.1 fusion.9
  2.1 0.0 copy-start.1
  2.1 0.1 fusion.8
  2.1 0.2 convolution_convert_fusion
  2.3 0.5 copy-done.1
  2.8 0.0 copy-start
  2.8 1.0 fusion.1.refs_0_
  3.8 0.0 copy-done
  3.8 153.7 %subspace.1 = (f32[64,256]{1,0:T(8,128)S(1)}, f32[64,64]{1,0:T(8,128)S(1)}) custom-call(bf16[608,256]{1,0:T(8,128)(2,1)S(1)} %fusion.1.refs_0_, f32[4]{0:T(128)S(1)} %copy-done), custom_call_target="tpu_custom_call" | custom-call | tf_op jit(solution)/shard_map/subspace/pallas_call | solution.py:431
  157.5 0.6 copy.10
  158.1 0.6 copy.11
  (3 shorter events, 0.0 us)
Async XLA Ops:
  1.3 0.7 copy-start.2
  2.1 0.8 copy-start.1
  2.8 1.0 copy-start

commit v2 on v1

--- a/solution.py
+++ b/solution.py
@@ -257,14 +257,27 @@
 
         return lax.fori_loop(1, half, body, carry)
 
+    def gather_early(step, buffer, use, carry):
+        def body(k, carry):
+            arrive(step, buffer, k)
+            forward(step, buffer, k)
+            carry = use(block_of(k - 1), carry)
+            arrive(step, buffer, half + k - 1)
+            return use(block_of(half + k - 1), carry)
+
+        carry = lax.fori_loop(1, half, body, carry)
+        carry = use(block_of(half - 1), carry)
+        arrive(step, buffer, 2 * half - 1)
+        return use(block_of(2 * half - 1), carry)
+
     begin(0, held)
     lanes = lax.broadcasted_iota(jnp.int32, (width, days), 1)
     turned = own[:days].astype(jnp.float32).T
-    shifted = [turned]
+    shifted = [2.0 * turned]
     for lag in range(1, lags):
-        shifted.append(jnp.where(lanes < days - lag, pltpu.roll(turned, days - lag, 1), 0.0))
-        shifted.append(jnp.where(lanes >= lag, pltpu.roll(turned, lag, 1), 0.0))
-    shifts = len(shifted)
+        later = jnp.where(lanes < days - lag, pltpu.roll(turned, days - lag, 1), 0.0)
+        earlier = jnp.where(lanes >= lag, pltpu.roll(turned, lag, 1), 0.0)
+        shifted.append(later + earlier)
     for i, part in enumerate(shifted):
         for q in range(2):
             stack[q, i * chunk : (i + 1) * chunk, :] = part[q * chunk : (q + 1) * chunk].astype(
@@ -276,12 +289,10 @@
         series = held[block, 0:days, :]
         for q in range(2):
             sums = jnp.dot(stack[q], series, preferred_element_type=jnp.float32)
-            rows = [sums[i * chunk : (i + 1) * chunk] for i in range(shifts)]
-            total = weights[0] * jnp.tanh(2 * BETA_CORR / days * rows[0])
+            soft = jnp.tanh(BETA_CORR / days * sums)
+            total = weights[0] * soft[:chunk]
             for lag in range(1, lags):
-                total += weights[lag] * jnp.tanh(
-                    BETA_CORR / days * (rows[2 * lag - 1] + rows[2 * lag])
-                )
+                total += weights[lag] * soft[lag * chunk : (lag + 1) * chunk]
             tiles[block, q * chunk : (q + 1) * chunk, :] = (tile_scale * total).astype(
                 jnp.bfloat16
             )
@@ -329,7 +340,7 @@
             out = out[:rank] + (out[rank : 2 * rank] + out[2 * rank :])
             return acc + counts[pl.ds(block, 1), :] * out
 
-        onward = gather(step + 1, buffer, multiply, zero)
+        onward = gather_early(step + 1, buffer, multiply, zero)
 
         if step == ITERS - 1:
             local_form = lax.dot_general(
@@ -358,7 +369,7 @@
                 inverse, onward, precision=HIGHEST, preferred_element_type=jnp.float32
             )
 
-    gather(ITERS + 1, forms, lambda block, carry: carry, jnp.int32(0))
+    gather_early(ITERS + 1, forms, lambda block, carry: carry, jnp.int32(0))
     packed = lax.fori_loop(0, n_blocks, lambda b, acc: acc + forms[b], zero_packed)
     left = jnp.dot(
         inverse, unpack(packed), precision=HIGHEST, preferred_element_type=jnp.float32
@@ -393,7 +404,7 @@
     return [
         ((n_blocks, held_rows, width), jnp.bfloat16),
         ((n_blocks, width, width), jnp.bfloat16),
-        ((2, (2 * lags - 1) * width // 2, days), jnp.bfloat16),
+        ((2, lags * width // 2, days), jnp.bfloat16),
         ((n_blocks, rank, width), jnp.float32),
         ((ITERS, n_blocks, rank + rank // 4, width), jnp.float32),
         ((n_blocks, rank // 4, width), jnp.float32),

time: 161 us -> 142 us (0.88)
  Pallas kernels: 154 us -> 136 us
    pallas_call x1, Pallas kernels: 154 us -> 136 us  [fused(): pl.pallas_call(body, out_shape=(jax.ShapeDtypeStruct((rank, width), jnp.f...]
where the time goes in v2:
time: 142 us; the launch traced here: 141 us
  Pallas kernels  136 us (96%)
  local copies, waits for them, and re-layouts  2.42 us (2%)
    pallas_call x1, Pallas kernels, fused(): pl.pallas_call(body, out_shape=(jax.ShapeDtypeStruct((rank, width), jnp.f...  136 us

profile of v2, /device:TPU:14, one launch (start us, length us, event | category | flops | bytes accessed | tf_op | source)
XLA Modules:
  0.0 140.8 jit_solution(3706053955300622417)
XLA Ops:
  1.3 0.0 copy-start.2
  1.3 0.7 copy-done.2
  2.0 0.1 fusion.9
  2.1 0.0 copy-start.1
  2.1 0.1 fusion.8
  2.1 0.2 convolution_convert_fusion
  2.3 0.5 copy-done.1
  2.8 0.0 copy-start
  2.8 1.0 fusion.1.refs_0_
  3.8 0.0 copy-done
  3.8 135.8 %subspace.1 = (f32[64,256]{1,0:T(8,128)S(1)}, f32[64,64]{1,0:T(8,128)S(1)}) custom-call(bf16[608,256]{1,0:T(8,128)(2,1)S(1)} %fusion.1.refs_0_, f32[4]{0:T(128)S(1)} %copy-done), custom_call_target="tpu_custom_call" | custom-call | tf_op jit(solution)/shard_map/subspace/pallas_call | solution.py:442
  139.6 0.6 copy.10
  140.2 0.6 copy.11
  (3 shorter events, 0.0 us)
Async XLA Ops:
  1.3 0.7 copy-start.2
  2.1 0.8 copy-start.1
  2.8 1.0 copy-start
